TPU v7x, 512 devices: a whole 4x8x8 slice. The times are simulated.
512 devices in a mesh: grp: 4 (over x), seq: 32 (over y_lo, z), rep: 4 (over y_hi, core).
Axes of the slice: x: 4, y: 8 (y_hi: 2, y_lo: 4; y = y_hi * 4 + y_lo), z: 8, core: 2. Of those that a mesh axis runs over, the one named last changes fastest.
Arguments:
- feature: bfloat16 [4, 4096, 16384], P('rep', None, ('grp', 'seq')), may hold values from -0.0234375 to 0.0234375
- cotangent: bfloat16 [4, 4096, 16384], P('rep', None, ('grp', 'seq')), may hold values from -6 to 6
- long_filter: bfloat16 [4096, 16384], P(None, ('grp', 'seq')), may hold values from -1 to 1
- short_filter: float32 [4096, 3], replicated, may hold values from -3 to 3
- skip_gain: float32 [4096], replicated, may hold values from -1 to 1
Outputs:
- input_grad: bfloat16 [4, 4096, 16384], P('rep', None, ('grp', 'seq'))
- filter_grad: float32 [4096, 16384], P('rep', ('grp', 'seq'))
- skip_grad: float32 [4096], replicated
All inputs are finite; a program needn't handle non-finite values.
Results may differ from a plain program's by a relative error of at most 0.012.
Values may be sent and summed in bfloat16 or wider, within the bound.
A program may use at most 64 MiB of HBM per device.

v0:
```python
import math

import jax
import jax.numpy as jnp
from jax import lax
from jax.experimental import pallas as pl
from jax.experimental.pallas import tpu as pltpu
from jax.sharding import PartitionSpec as P

def tables(n):
    p = jnp.arange(n, dtype=jnp.int32)
    def cis(num, den):
        ang = (num % den).astype(jnp.float32) * (2.0 * math.pi / den)
        return jnp.cos(ang), -jnp.sin(ang)
    quarter = 4 * p + 1
    o_re, o_im = cis(quarter[:, None] * p[None, :], 4 * n)
    t_re, t_im = cis(quarter[:, None] * p[None, :], 4 * n * n)
    i_re, i_im = cis(p[:, None] * p[None, :], n)
    bf = jnp.bfloat16
    fwd_outer = jnp.concatenate([o_re, o_im], 0).astype(bf)
    fwd_inner = jnp.concatenate([jnp.concatenate([i_re, i_im], 1), jnp.concatenate([-i_im, i_re], 1)], 0).astype(bf)
    inv_inner = jnp.concatenate([jnp.concatenate([i_re, -i_im], 1), jnp.concatenate([i_im, i_re], 1)], 0).astype(bf)
    inv_outer = (jnp.concatenate([o_re.T, o_im.T], 1) * (1.0 / (n * n))).astype(bf)
    return fwd_outer, t_re, t_im, fwd_inner, inv_inner, inv_outer

def core(x_ref, h_ref, taps_ref, fo_ref, tr_ref, ti_ref, fi_ref, ii_ref, io_ref, ig_ref, fg_ref, sk_ref,
         xs, hs, os, gs, bs, ys, zs, ds):
    n = 128; nb = 4; ch = 8
    f32, bf = jnp.float32, jnp.bfloat16
    def expand(k, _):
        xs[pl.ds(pl.multiple_of(k*256,256), 256), :] = x_ref[pl.ds(k*16,16)].astype(f32).reshape(256, n)
        return 0
    lax.fori_loop(0, 32, expand, 0)
    def expand_h(k, _):
        hs[pl.ds(pl.multiple_of(k*256,256), 256), :] = h_ref[pl.ds(k*16,16)].astype(f32).reshape(256, n)
        return 0
    lax.fori_loop(0, 4, expand_h, 0)
    lane = lax.broadcasted_iota(jnp.int32, (n, n), 1)
    row = lax.broadcasted_iota(jnp.int32, (n, n), 0)

    def shifted(v, m):
        here = pltpu.roll(v, n - m, 1)
        below = jnp.where(row == n - 1, 0.0, pltpu.roll(here, n - 1, 0))
        return jnp.where(lane >= n - m, below, here)

    def channel(c, _):
        sk = jnp.zeros((8, n), f32)
        for b in range(nb):
            feat = xs[pl.ds(b*16 + c, n, stride=64), :]
            cot = xs[pl.ds(b*16 + 8 + c, n, stride=64), :]
            ds[:, b*n:(b+1)*n] = feat.astype(bf)
            ds[:, (nb+b)*n:(nb+b+1)*n] = cot.astype(bf)
            sk = sk + jnp.sum((feat*cot).reshape(16, 8, n), axis=0)
        ds[:, 2*nb*n:] = hs[pl.ds(c, n, stride=8), :].astype(bf)
        sk_ref[pl.ds(c, 1), :] = jnp.sum(sk, axis=0, keepdims=True)
        first = jnp.dot(fo_ref[...], ds[...], preferred_element_type=f32)
        tr, ti = tr_ref[...], ti_ref[...]
        for s in range(2*nb+1):
            re = first[:n, s*n:(s+1)*n]; im = first[n:, s*n:(s+1)*n]
            bs[s*n:(s+1)*n, :n] = (re*tr - im*ti).astype(bf)
            bs[s*n:(s+1)*n, n:] = (re*ti + im*tr).astype(bf)
        spec = jnp.dot(bs[...], fi_ref[...], preferred_element_type=f32)
        h_re, h_im = spec[2*nb*n:, :n], spec[2*nb*n:, n:]
        g_re = jnp.zeros((n, n), f32); g_im = jnp.zeros((n, n), f32)
        for b in range(nb):
            f_re, f_im = spec[b*n:(b+1)*n, :n], spec[b*n:(b+1)*n, n:]
            c_re, c_im = spec[(nb+b)*n:(nb+b+1)*n, :n], spec[(nb+b)*n:(nb+b+1)*n, n:]
            ys[b*n:(b+1)*n, :n] = (h_re*c_re + h_im*c_im).astype(bf)
            ys[b*n:(b+1)*n, n:] = (h_re*c_im - h_im*c_re).astype(bf)
            g_re += f_re*c_re + f_im*c_im
            g_im += f_re*c_im - f_im*c_re
        ys[nb*n:, :n] = g_re.astype(bf)
        ys[nb*n:, n:] = g_im.astype(bf)
        back = jnp.dot(ys[...], ii_ref[...], preferred_element_type=f32)
        for s in range(nb+1):
            re = back[s*n:(s+1)*n, :n]; im = back[s*n:(s+1)*n, n:]
            zs[:n, s*n:(s+1)*n] = (re*tr + im*ti).astype(bf)
            zs[n:, s*n:(s+1)*n] = (im*tr - re*ti).astype(bf)
        out = jnp.dot(io_ref[...], zs[...], preferred_element_type=f32)
        gs[pl.ds(c, n, stride=8), :] = out[:, nb*n:]
        for b in range(nb):
            cot = xs[pl.ds(b*16 + 8 + c, n, stride=64), :]
            total = out[:, b*n:(b+1)*n] + taps_ref[c, 3]*cot
            res = taps_ref[c, 0]*total + taps_ref[c, 1]*shifted(total, 1) + taps_ref[c, 2]*shifted(total, 2)
            os[pl.ds(b*8 + c, n, stride=32), :] = res
        return 0
    lax.fori_loop(0, ch, channel, 0)
    def pack(k, _):
        ig_ref[pl.ds(k*16,16)] = os[pl.ds(pl.multiple_of(k*256,256), 256), :].reshape(16, 16, n).astype(bf)
        return 0
    lax.fori_loop(0, 16, pack, 0)
    def pack_g(k, _):
        fg_ref[pl.ds(k*16,16)] = gs[pl.ds(pl.multiple_of(k*256,256), 256), :].reshape(16, 16, n).astype(bf)
        return 0
    lax.fori_loop(0, 4, pack_g, 0)

def scratch():
    n=128
    return [pltpu.VMEM((8192,n),jnp.float32), pltpu.VMEM((1024,n),jnp.float32), pltpu.VMEM((4096,n),jnp.float32),
      pltpu.VMEM((1024,n),jnp.float32), pltpu.VMEM((9*n,2*n),jnp.bfloat16), pltpu.VMEM((5*n,2*n),jnp.bfloat16),
      pltpu.VMEM((2*n,5*n),jnp.bfloat16), pltpu.VMEM((n,9*n),jnp.bfloat16)]


def transform(x, h, taps):
    vm = pl.BlockSpec(memory_space=pltpu.VMEM)
    return pl.pallas_call(core,
      out_shape=(jax.ShapeDtypeStruct((256,16,128),jnp.bfloat16),jax.ShapeDtypeStruct((64,16,128),jnp.bfloat16),jax.ShapeDtypeStruct((8,128),jnp.float32)),
      in_specs=[vm,vm,pl.BlockSpec(memory_space=pltpu.SMEM)]+[vm]*6, out_specs=(vm,vm,vm),
      scratch_shapes=scratch(),
      compiler_params=pltpu.CompilerParams(vmem_limit_bytes=40<<20))(x,h,taps,*tables(128))


def body(feature, cotangent, long_filter, short_filter, skip_gain):
    rep = lax.axis_index("rep")
    owner = rep * 128 + lax.axis_index("grp") * 32 + lax.axis_index("seq")
    both = jnp.stack([feature[0].reshape(4, 128, 8, 128), cotangent[0].reshape(4, 128, 8, 128)], 2)
    both = both.transpose(1, 0, 2, 3, 4).reshape(512, 16, 128)
    x = lax.all_to_all(both, ("grp", "seq", "rep"), 0, 0, tiled=True)
    filt = lax.dynamic_slice_in_dim(long_filter, rep * 1024, 1024, 0).reshape(128, 8, 128)
    h = lax.all_to_all(filt, ("grp", "seq"), 0, 0, tiled=True).reshape(64, 16, 128)
    taps = jnp.concatenate([short_filter, skip_gain[:, None]], 1)
    taps = lax.dynamic_slice_in_dim(taps, owner * 8, 8, 0)
    ig, fg, sk = transform(x, h, taps)
    ig = lax.all_to_all(ig.reshape(512, 8, 128), ("grp", "seq", "rep"), 0, 0, tiled=True)
    ig = ig.reshape(128, 4, 8, 128).transpose(1, 0, 2, 3).reshape(1, 4096, 128)
    fg = lax.all_to_all(fg.reshape(128, 8, 128), ("grp", "seq"), 0, 0, tiled=True)
    fg = fg.reshape(1024, 128).astype(jnp.float32)
    sk = lax.all_gather(jnp.sum(sk, axis=1), ("rep", "grp", "seq"), tiled=True)
    return ig, fg, sk


def solution(mesh):
    return jax.shard_map(
        body,
        mesh=mesh,
        in_specs=(
            P("rep", None, ("grp", "seq")),
            P("rep", None, ("grp", "seq")),
            P(None, ("grp", "seq")),
            P(),
            P(),
        ),
        out_specs=(P("rep", None, ("grp", "seq")), P("rep", ("grp", "seq")), P()),
        check_vma=False,
    )
```

profile of v0, /device:TPU:1, one launch (start us, length us, event | category | flops | bytes accessed | tf_op | source)
XLA Modules:
  0.0 267.2 jit_solution(13931646434333337685)
XLA Ops:
  0.6 0.0 copy-start
  0.7 1.2 copy-done
  1.9 0.7 dynamic-slice_bitcast_fusion
  2.6 18.6 %all-to-all-start.1 = ((bf16[128,8,128]{2,1,0:T(8,128)(2,1)}), bf16[128,8,128]{2,1,0:T(8,128)(2,1)S(1)}, u32[]{:S(2)}, u32[]{:S(2)}) async-start(bf16[128,8,128]{2,1,0:T(8,128)(2,1)} %dynamic-slice_bitcast_fusion), calls=%async_computation.1 | async-start | bytes 524288 | tf_op jit(solution)/shard_map/all_to_all | solution.py:120
  21.2 1.7 pad_maximum_fusion
  22.9 1.9 copy.21
  24.8 9.4 %all-to-all-done.1 = bf16[128,8,128]{2,1,0:T(8,128)(2,1)S(1)} async-done(((bf16[128,8,128]{2,1,0:T(8,128)(2,1)}), bf16[128,8,128]{2,1,0:T(8,128)(2,1)S(1)}, u32[]{:S(2)}, u32[]{:S(2)}) %all-to-all-start.1) | async-done | bytes 262176 | tf_op jit(solution)/shard_map/all_to_all | solution.py:120
  34.2 0.0 copy-start.7
  34.2 0.0 copy-start.8
  34.2 10.5 %all-to-all-start = ((bf16[512,16,128]{2,1,0:T(8,128)(2,1)}), bf16[512,16,128]{2,1,0:T(8,128)(2,1)S(1)}, u32[]{:S(2)}, u32[]{:S(2)}) async-start(bf16[512,16,128]{2,1,0:T(8,128)(2,1)} %bitcast.22), calls=%async_computation | async-start | bytes 4194304 | tf_op jit(solution)/shard_map/all_to_all | solution.py:118
  44.8 0.0 copy-done.7
  44.8 0.0 copy-done.8
  44.8 0.1 fusion.30
  44.9 0.1 copy.22.taps_ref
  45.0 0.3 fusion.27
  45.2 0.3 negate_convert_fusion
  45.5 1.5 fusion.28
  47.0 0.6 pad_maximum_fusion.5.fo_ref
  47.6 0.6 fusion.2.io_ref
  48.2 0.7 fusion.1
  48.9 51.2 %all-to-all-done.x_ref = bf16[512,16,128]{2,1,0:T(8,128)(2,1)S(1)} async-done(((bf16[512,16,128]{2,1,0:T(8,128)(2,1)}), bf16[512,16,128]{2,1,0:T(8,128)(2,1)S(1)}, u32[]{:S(2)}, u32[]{:S(2)}) %all-to-all-start) | async-done | bytes 2097184 | tf_op jit(solution)/shard_map/all_to_all | solution.py:118
  100.1 0.0 copy-start.2
  100.1 0.9 copy-done.2
  101.0 0.0 copy-start.3
  101.0 0.8 copy-done.3
  101.9 0.0 copy-start.4
  101.9 0.8 copy-done.4
  102.7 0.0 copy-start.5
  102.7 0.8 copy-done.5
  103.5 0.0 copy-start.6
  103.5 0.8 copy-done.6
  104.4 14.4 %shard_map.76 = (bf16[256,16,128]{2,1,0:T(8,128)(2,1)S(1)}, bf16[64,16,128]{2,1,0:T(8,128)(2,1)S(1)}, f32[8,128]{1,0:T(8,128)S(1)}) custom-call(bf16[512,16,128]{2,1,0:T(8,128)(2,1)S(1)} %all-to-all-done.x_ref, bf16[64,16,128]{2,1,0:T(8,128)(2,1)S(1)} %bitcast.20, f32[8,4]{1,0:T(8,128)S(1)} %copy.22.taps_ref, bf16[256,128]{1,0:T(8,128)(2,1)S(1)} %copy-done.6, ...), custom_call_target="tpu_custom_call" | custom-call | tf_op jit(solution)/shard_map/pallas_call | solution.py:106
  118.8 0.0 copy-start.1
  118.8 1.0 copy-done.1
  119.7 20.9 %all_to_all.20 = bf16[128,8,128]{2,1,0:T(8,128)(2,1)S(1)} all-to-all(bf16[128,8,128]{2,1,0:T(8,128)(2,1)S(1)} %bitcast.21), channel_id=1, replica_groups=mesh['grp'=4,'seq'=32,'rep'=4] {'grp','seq'}, dimensions={0} | all-to-all | bytes 524288 | tf_op jit(solution)/shard_map/all_to_all | solution.py:126
  140.6 10.2 %all-to-all-start.2 = ((bf16[512,8,128]{2,1,0:T(8,128)(2,1)}), bf16[512,8,128]{2,1,0:T(8,128)(2,1)S(1)}, u32[]{:S(2)}, u32[]{:S(2)}) async-start(bf16[512,8,128]{2,1,0:T(8,128)(2,1)} %bitcast.19), calls=%async_computation.2 | async-start | bytes 2097152 | tf_op jit(solution)/shard_map/all_to_all | solution.py:124
  150.8 1.3 dynamic-slice
  152.7 0.1 reduce_sum.9
  152.8 0.3 dynamic-update-slice
  153.1 112.1 %all-reduce = f32[4096]{0:T(1024)} all-reduce(f32[4096]{0:T(1024)S(1)} %dynamic-update-slice), channel_id=1, replica_groups=mesh['grp'=4,'seq'=32,'rep'=4] {'rep','grp','seq'}, use_global_device_ids=true, to_apply=%add | all-reduce | flops 4096 | bytes 32768
  265.2 0.8 bitcast_convert_fusion
  266.1 0.0 all-to-all-done.2
  266.1 1.2 copy.20
  (2 shorter events, 0.0 us)
Async XLA Ops:
  0.6 1.2 copy-start
  2.6 31.6 %all-to-all-start.1 = ((bf16[128,8,128]{2,1,0:T(8,128)(2,1)}), bf16[128,8,128]{2,1,0:T(8,128)(2,1)S(1)}, u32[]{:S(2)}, u32[]{:S(2)}) async-start(bf16[128,8,128]{2,1,0:T(8,128)(2,1)} %dynamic-slice_bitcast_fusion), calls=%async_computation.1 | async-start | bytes 524288 | tf_op jit(solution)/shard_map/all_to_all | solution.py:120
  34.2 10.6 %copy-start.7 = (f32[4096,3]{0,1:T(4,128)S(1)}, f32[4096,3]{0,1:T(4,128)}, u32[]{:S(2)}) copy-start(f32[4096,3]{0,1:T(4,128)} %param.8) | copy-start | bytes 147460
  34.2 10.6 %copy-start.8 = (f32[4096]{0:T(1024)S(1)}, f32[4096]{0:T(1024)}, u32[]{:S(2)}) copy-start(f32[4096]{0:T(1024)} %param.9) | copy-start | bytes 49156
  34.2 65.9 %all-to-all-start = ((bf16[512,16,128]{2,1,0:T(8,128)(2,1)}), bf16[512,16,128]{2,1,0:T(8,128)(2,1)S(1)}, u32[]{:S(2)}, u32[]{:S(2)}) async-start(bf16[512,16,128]{2,1,0:T(8,128)(2,1)} %bitcast.22), calls=%async_computation | async-start | bytes 4194304 | tf_op jit(solution)/shard_map/all_to_all | solution.py:118
  100.1 0.9 copy-start.2
  101.0 0.8 copy-start.3
  101.9 0.8 copy-start.4
  102.7 0.8 copy-start.5
  103.5 0.8 copy-start.6
  118.8 1.0 copy-start.1
  140.6 125.5 %all-to-all-start.2 = ((bf16[512,8,128]{2,1,0:T(8,128)(2,1)}), bf16[512,8,128]{2,1,0:T(8,128)(2,1)S(1)}, u32[]{:S(2)}, u32[]{:S(2)}) async-start(bf16[512,8,128]{2,1,0:T(8,128)(2,1)} %bitcast.19), calls=%async_computation.2 | async-start | bytes 2097152 | tf_op jit(solution)/shard_map/all_to_all | solution.py:124
where the time goes:
time: 269 us; the launch traced here: 267 us
  blocking collectives  133 us (49%)
  waiting for transfers between devices  60.6 us (23%)
  starting transfers between devices  39.3 us (15%)
  Pallas kernels  14.4 us (5%)
  local copies, waits for them, and re-layouts  11.9 us (4%)
  other arithmetic  6.7 us (2%)
    unnamed x1, blocking collectives  112 us
    all_to_all x1, waiting for transfers between devices, body(): x = lax.all_to_all(both, ('grp', 'seq', 'rep'), 0, 0, tiled=True)  51.2 us
    all_to_all x1, blocking collectives, body(): lax.all_to_all(fg.reshape(128, 8, 128), ('grp', 'seq'), 0, 0, tiled=True)  20.9 us
    all_to_all x1, starting transfers between devices, body(): lax.all_to_all(filt, ('grp', 'seq'), 0, 0, tiled=True).reshape(64, 16, 128)  18.6 us
    pallas_call x1, Pallas kernels, transform(): pl.pallas_call(core, out_shape=(jax.ShapeDtypeStruct((256, 16, 128), jnp....  14.4 us
    all_to_all x1, starting transfers between devices, body(): x = lax.all_to_all(both, ('grp', 'seq', 'rep'), 0, 0, tiled=True)  10.5 us
    all_to_all x1, starting transfers between devices, body(): lax.all_to_all(ig.reshape(512, 8, 128), ('grp', 'seq', 'rep'), 0, 0, tile...  10.2 us
    all_to_all x1, waiting for transfers between devices, body(): lax.all_to_all(filt, ('grp', 'seq'), 0, 0, tiled=True).reshape(64, 16, 128)  9.38 us
  transfers between devices with their start and end apart: 3, of which 2 were waited for; matrix products, arithmetic and copies ran while one was open for 4% of the time, Pallas kernels for 0%

commit v1 on v0

v1 whole, which is shorter than its diff:
```python
import math

import jax
import jax.numpy as jnp
from jax import lax
from jax.experimental import pallas as pl
from jax.experimental.pallas import tpu as pltpu
from jax.sharding import PartitionSpec as P

MESH = pl.DeviceIdType.MESH
rem, div = lax.rem, lax.div
Z, V, R = 8, 16, 4
W = R * V
N = 128
F32, BF = jnp.float32, jnp.bfloat16
ZORDER = (4, 3, 5, 2, 6, 1, 7)
MIX = 27


def tables(n):
    p = jnp.arange(n, dtype=jnp.int32)
    def cis(num, den):
        ang = (num % den).astype(jnp.float32) * (2.0 * math.pi / den)
        return jnp.cos(ang), -jnp.sin(ang)
    quarter = 4 * p + 1
    o_re, o_im = cis(quarter[:, None] * p[None, :], 4 * n)
    t_re, t_im = cis(quarter[:, None] * p[None, :], 4 * n * n)
    i_re, i_im = cis(p[:, None] * p[None, :], n)
    bf = jnp.bfloat16
    fwd_outer = jnp.concatenate([o_re, o_im], 0).astype(bf)
    fwd_inner = jnp.concatenate([jnp.concatenate([i_re, i_im], 1), jnp.concatenate([-i_im, i_re], 1)], 0).astype(bf)
    inv_inner = jnp.concatenate([jnp.concatenate([i_re, -i_im], 1), jnp.concatenate([i_im, i_re], 1)], 0).astype(bf)
    inv_outer = (jnp.concatenate([o_re.T, o_im.T], 1) * (1.0 / (n * n))).astype(bf)
    return fwd_outer, t_re, t_im, fwd_inner, inv_inner, inv_outer


def place():
    g = lax.axis_index("grp")
    s = lax.axis_index("seq")
    r = lax.axis_index("rep")
    return g, div(r, 2) * 4 + div(s, Z), rem(s, Z), rem(r, 2)


def plane_id(x, y, core):
    return (div(y, 4) * 2 + core) * V + x * 4 + rem(y, 4)


def z_mate(k, me):
    to = rem(me[2] + k, Z)
    return to, {"seq": rem(me[1], 4) * Z + to}


def plane_device(x, y, core, me):
    return {"grp": x, "seq": rem(y, 4) * Z + me[2], "rep": div(y, 4) * 2 + core}


def w_mate(k, me):
    x = rem(me[0] + rem(k, 4), 4)
    core = rem(me[3] + rem(div(k, 4), 2), 2)
    y = rem(me[1] + div(k, 8), 8)
    return plane_id(x, y, core), plane_device(x, y, core, me)


def core_mate(k, core, me):
    x = rem(me[0] + rem(k, 4), 4)
    y = rem(me[1] + div(k, 4), 8)
    return div(y, 4) * V + x * 4 + rem(y, 4), plane_device(x, y, core, me)


def v_mate(k, me):
    x = rem(me[0] + rem(k, 4), 4)
    low = rem(rem(me[1], 4) + div(k, 4), 4)
    return x * 4 + low, {"grp": x, "seq": low * Z + me[2]}


def each(lo, hi, f):
    def step(k, carry):
        f(k)
        return carry

    lax.fori_loop(lo, hi, step, 0)


def greet(me):
    barrier = pltpu.get_barrier_semaphore()

    def signal(device):
        pl.semaphore_signal(barrier, inc=1, device_id=device, device_id_type=MESH)

    each(1, Z, lambda k: signal(z_mate(k, me)[1]))
    each(1, W, lambda k: signal(w_mate(k, me)[1]))
    pl.semaphore_wait(barrier, Z + W - 2)


def done(ref, sem):
    pltpu.make_async_copy(ref, ref, sem).wait()


def gather_inputs(me, f_ref, c_ref, h_ref, fx, cx, hx, ia, ib, ih, send, recv, loc):
    z = me[2]
    w = plane_id(me[0], me[1], me[3])
    r, v = div(w, V), rem(w, V)

    def remote(src, dst, i, device):
        pltpu.make_async_remote_copy(
            src, dst, send.at[i], recv.at[i], device_id=device, device_id_type=MESH
        ).start()

    def local(src, dst, i):
        copy = pltpu.make_async_copy(src, dst, loc.at[i])
        copy.start()
        return copy

    own = [
        local(f_ref.at[:, z], ia.at[z], 0),
        local(c_ref.at[r, :, v], ib.at[w], 1),
        local(h_ref.at[r, z], ih.at[z], 2),
    ]

    def cot_plane(k):
        to, device = w_mate(rem(k * MIX, W), me)
        remote(c_ref.at[div(to, V), :, rem(to, V)], ib.at[w], 1, device)

    for k in ZORDER:
        to, device = z_mate(k, me)
        remote(f_ref.at[:, to], ia.at[z], 0, device)
        remote(h_ref.at[r, to], ih.at[z], 4, device)
    each(1, W, cot_plane)
    for copy in own:
        copy.wait()
    done(ih.at[pl.ds(0, Z - 1)], recv.at[4])
    own_h = local(ih.at[:, v], hx.at[v], 0)

    def filt_plane(k):
        to, device = v_mate(k, me)
        remote(ih.at[:, to], hx.at[v], 5, device)

    each(1, V, filt_plane)
    done(ia.at[pl.ds(0, Z - 1)], recv.at[0])
    own_f = local(ia.at[:, r, v], fx.at[w], 1)

    def feat_plane(k):
        to, device = w_mate(rem(k * MIX, W), me)
        remote(ia.at[:, div(to, V), rem(to, V)], fx.at[w], 2, device)

    each(1, W, feat_plane)
    done(ib.at[pl.ds(0, W - 1)], recv.at[1])
    own_c = local(ib.at[:, z], cx.at[:, z], 2)
    for k in ZORDER:
        to, device = z_mate(k, me)
        remote(ib.at[:, to], cx.at[:, z], 3, device)
    own_h.wait()
    own_f.wait()
    own_c.wait()
    for i in (0, 1, 2, 3):
        done(fx.at[pl.ds(0, W - 1)] if i in (1, 2) else cx.at[:, pl.ds(0, Z - 1)], send.at[i])
    done(ih.at[pl.ds(0, Z - 1)], send.at[4])
    done(hx.at[pl.ds(0, V - 1)], send.at[5])
    done(hx.at[pl.ds(0, V - 1)], recv.at[5])
    done(fx.at[pl.ds(0, W - 1)], recv.at[2])
    done(cx.at[:, pl.ds(0, Z - 1)], recv.at[3])


def shifted(values, m):
    lane = lax.broadcasted_iota(jnp.int32, (N, N), 1)
    row = lax.broadcasted_iota(jnp.int32, (N, N), 0)
    here = pltpu.roll(values, N - m, 1)
    below = jnp.where(row == N - 1, 0.0, pltpu.roll(here, N - 1, 0))
    return jnp.where(lane >= N - m, below, here)


def transform(me, fx, cx, hx, taps_ref, tabs, oa, ob, go, sk, fs, cs, hs, os, gs, ds, bs, ys, zs):
    fo_ref, tr_ref, ti_ref, fi_ref, ii_ref, io_ref = tabs
    rows = Z * 8

    def expand(w):
        at = pl.ds(pl.multiple_of(w * rows, rows), rows)
        fs[at, :] = fx[w].astype(F32).reshape(rows, N)
        cs[at, :] = cx[w].astype(F32).reshape(rows, N)

    each(0, W, expand)

    def expand_h(v):
        hs[pl.ds(pl.multiple_of(v * rows, rows), rows), :] = hx[v].astype(F32).reshape(rows, N)

    each(0, V, expand_h)
    sk[...] = jnp.zeros((1, N), F32)
    sig_c, sig_h = R, 2 * R

    def channel(c):
        total = jnp.zeros((8, N), F32)
        for b in range(R):
            feat = fs[pl.ds(b * 8 * N + c, N, stride=8), :]
            cot = cs[pl.ds(b * 8 * N + c, N, stride=8), :]
            ds[:, b * N:(b + 1) * N] = feat.astype(BF)
            ds[:, (sig_c + b) * N:(sig_c + b + 1) * N] = cot.astype(BF)
            total = total + jnp.sum((feat * cot).reshape(N // 8, 8, N), axis=0)
        ds[:, sig_h * N:] = hs[pl.ds(c, N, stride=8), :].astype(BF)
        total = jnp.sum(jnp.sum(total, axis=0, keepdims=True), axis=1, keepdims=True)
        lane = lax.broadcasted_iota(jnp.int32, (1, N), 1)
        sk[...] += jnp.where(lane == me[2] * 8 + c, total, 0.0)
        first = jnp.dot(fo_ref[...], ds[...], preferred_element_type=F32)
        tr, ti = tr_ref[...], ti_ref[...]
        for s in range(2 * R + 1):
            re, im = first[:N, s * N:(s + 1) * N], first[N:, s * N:(s + 1) * N]
            bs[s * N:(s + 1) * N, :N] = (re * tr - im * ti).astype(BF)
            bs[s * N:(s + 1) * N, N:] = (re * ti + im * tr).astype(BF)
        spec = jnp.dot(bs[...], fi_ref[...], preferred_element_type=F32)

        def part(s):
            return spec[s * N:(s + 1) * N, :N], spec[s * N:(s + 1) * N, N:]

        h_re, h_im = part(sig_h)
        g_re = jnp.zeros((N, N), F32)
        g_im = jnp.zeros((N, N), F32)
        for b in range(R):
            f_re, f_im = part(b)
            c_re, c_im = part(sig_c + b)
            ys[b * N:(b + 1) * N, :N] = (h_re * c_re + h_im * c_im).astype(BF)
            ys[b * N:(b + 1) * N, N:] = (h_re * c_im - h_im * c_re).astype(BF)
            g_re += f_re * c_re + f_im * c_im
            g_im += f_re * c_im - f_im * c_re
        ys[R * N:, :N] = g_re.astype(BF)
        ys[R * N:, N:] = g_im.astype(BF)
        back = jnp.dot(ys[...], ii_ref[...], preferred_element_type=F32)
        for s in range(R + 1):
            re, im = back[s * N:(s + 1) * N, :N], back[s * N:(s + 1) * N, N:]
            zs[:N, s * N:(s + 1) * N] = (re * tr + im * ti).astype(BF)
            zs[N:, s * N:(s + 1) * N] = (im * tr - re * ti).astype(BF)
        out = jnp.dot(io_ref[...], zs[...], preferred_element_type=F32)
        gs[pl.ds(c, N, stride=8), :] = out[:, R * N:]
        for b in range(R):
            cot = cs[pl.ds(b * 8 * N + c, N, stride=8), :]
            grad = out[:, b * N:(b + 1) * N] + taps_ref[c, 3] * cot
            res = (
                taps_ref[c, 0] * grad
                + taps_ref[c, 1] * shifted(grad, 1)
                + taps_ref[c, 2] * shifted(grad, 2)
            )
            os[pl.ds(b * 8 * N + c, N, stride=8), :] = res

    each(0, 8, channel)

    def pack(q):
        half, v = div(q, V), rem(q, V)
        base = (half * 2) * 8 * N + v * rows
        for z in range(Z):
            oa[z, q] = os[pl.ds(pl.multiple_of(base + z * 8, 8), 8), :].astype(BF)
        base = base + 8 * N
        ob[q] = os[pl.ds(pl.multiple_of(base, rows), rows), :].reshape(Z, 8, N).astype(BF)

    each(0, W // 2, pack)

    def pack_g(v):
        for z in range(Z):
            go[z, v] = gs[pl.ds(pl.multiple_of(v * rows + z * 8, 8), 8), :].astype(BF)

    each(0, V, pack_g)


def scatter_outputs(me, oa, ob, go, sk, out, out_g, out_s, ia, ib, tally, ig, si, mid, send, recv, loc):
    z, core = me[2], me[3]
    w = plane_id(me[0], me[1], core)
    r, v = div(w, V), rem(w, V)
    q = div(r, 2) * V + v

    def remote(src, dst, i, device):
        pltpu.make_async_remote_copy(
            src, dst, send.at[i], recv.at[i], device_id=device, device_id_type=MESH
        ).start()

    def local(src, dst, i):
        copy = pltpu.make_async_copy(src, dst, loc.at[i])
        copy.start()
        return copy

    def one_plane(k):
        to, device = core_mate(rem(k * MIX, W // 2), 1, me)
        remote(ob.at[to], ib.at[r, v], 8, device)

    own = [local(oa.at[z], ia.at[z], 0), local(go.at[z], ig.at[z], 1), local(sk, si.at[z], 2)]
    for k in ZORDER:
        to, device = z_mate(k, me)
        remote(oa.at[to], ia.at[z], 6, device)
        remote(go.at[to], ig.at[z], 10, device)
        remote(sk, si.at[z], 12, device)
    each(core, W // 2, one_plane)
    for copy in own:
        copy.wait()

    @pl.when(core == 1)
    def _():
        local(ob.at[q], ib.at[r, v], 0).wait()

    done(si.at[pl.ds(0, Z - 1)], recv.at[12])
    mid[...] = jnp.sum(si[...], axis=0)
    own_s = local(mid, out_s.at[w], 2)

    def sums_plane(k):
        to, device = w_mate(rem(k * MIX, W), me)
        remote(mid, out_s.at[w], 13, device)

    each(1, W, sums_plane)
    done(ia.at[pl.ds(0, Z - 1)], recv.at[6])

    @pl.when(core == 0)
    def _():
        local(ia.at[:, q], out.at[r, :, v], 0).wait()

    def zero_plane(k):
        to, device = core_mate(rem(k * MIX, W // 2), 0, me)
        remote(ia.at[:, to], out.at[r, :, v], 7, device)

    each(1 - core, W // 2, zero_plane)
    done(ig.at[pl.ds(0, Z - 1)], recv.at[10])
    own_g = local(ig.at[:, v], out_g.at[:, v], 1)

    def grad_plane(k):
        to, device = v_mate(k, me)
        remote(ig.at[:, to], out_g.at[:, v], 11, device)

    each(1, V, grad_plane)

    @pl.when(core == 1)
    def _():
        done(tally.at[pl.ds(0, W - 1)], recv.at[8])
        own_b = local(ib.at[:, :, z], out.at[:, z], 0)
        for k in ZORDER:
            to, device = z_mate(k, me)
            remote(ib.at[:, :, to], out.at[:, z], 9, device)
        own_b.wait()
        done(tally.at[:, pl.ds(0, Z - 1)], send.at[9])
        done(tally.at[pl.ds(0, W // 2 - 1)], send.at[8])
        done(tally.at[pl.ds(0, W // 2)], send.at[7])
        done(tally.at[:, pl.ds(0, Z - 1)], recv.at[9])

    @pl.when(core == 0)
    def _():
        done(tally.at[pl.ds(0, W // 2)], send.at[8])
        done(tally.at[pl.ds(0, W // 2 - 1)], send.at[7])
        done(tally.at[pl.ds(0, W - 1)], recv.at[7])

    own_s.wait()
    own_g.wait()
    done(ia.at[pl.ds(0, Z - 1)], send.at[6])
    done(ig.at[pl.ds(0, Z - 1)], send.at[10])
    done(out_g.at[:, pl.ds(0, V - 1)], send.at[11])
    done(out_g.at[:, pl.ds(0, V - 1)], recv.at[11])
    done(si.at[pl.ds(0, Z - 1)], send.at[12])
    done(out_s.at[pl.ds(0, W - 1)], send.at[13])
    done(out_s.at[pl.ds(0, W - 1)], recv.at[13])


def kernel(
    f_ref, c_ref, h_ref, taps_ref, fo_ref, tr_ref, ti_ref, fi_ref, ii_ref, io_ref,
    out, out_g, out_s,
    ia, ib, ih, fx, cx, hx, fs, cs, hs, os, gs, ds, bs, ys, zs,
    oa, ob, go, sk, ia2, ib2, ig2, si, mid, send, recv, loc,
):
    me = place()
    greet(me)
    gather_inputs(me, f_ref, c_ref, h_ref, fx, cx, hx, ia, ib, ih, send, recv, loc)
    tabs = (fo_ref, tr_ref, ti_ref, fi_ref, ii_ref, io_ref)
    transform(me, fx, cx, hx, taps_ref, tabs, oa, ob, go, sk, fs, cs, hs, os, gs, ds, bs, ys, zs)
    scatter_outputs(me, oa, ob, go, sk, out, out_g, out_s, ia2, ib2, fx, ig2, si, mid, send, recv, loc)


def run(feature, cotangent, long_filter, taps):
    def bf(*shape):
        return pltpu.VMEM(shape + (8, N), BF)

    def f32(*shape):
        return pltpu.VMEM(shape, F32)

    vm = pl.BlockSpec(memory_space=pltpu.VMEM)
    whole = pl.BlockSpec(memory_space=pl.ANY)
    return pl.pallas_call(
        kernel,
        out_shape=(
            jax.ShapeDtypeStruct((R, Z, V, 8, N), BF),
            jax.ShapeDtypeStruct((Z, V, 8, N), BF),
            jax.ShapeDtypeStruct((W, 1, N), F32),
        ),
        in_specs=[whole] * 3 + [pl.BlockSpec(memory_space=pltpu.SMEM)] + [vm] * 6,
        out_specs=(vm, vm, vm),
        scratch_shapes=[
            bf(Z, R, V), bf(W, Z), bf(Z, V), bf(W, Z), bf(W, Z), bf(V, Z),
            f32(W * Z * 8, N), f32(W * Z * 8, N), f32(V * Z * 8, N), f32(W * Z * 8, N), f32(V * Z * 8, N),
            pltpu.VMEM((N, 9 * N), BF), pltpu.VMEM((9 * N, 2 * N), BF),
            pltpu.VMEM((5 * N, 2 * N), BF), pltpu.VMEM((2 * N, 5 * N), BF),
            bf(Z, W // 2), bf(W // 2, Z), bf(Z, V), f32(1, N),
            bf(Z, W // 2), bf(R, V, Z), bf(Z, V), f32(Z, 1, N), f32(1, N),
            pltpu.SemaphoreType.DMA((14,)), pltpu.SemaphoreType.DMA((14,)), pltpu.SemaphoreType.DMA((3,)),
        ],
        compiler_params=pltpu.CompilerParams(
            collective_id=0, has_side_effects=True, vmem_limit_bytes=48 << 20
        ),
    )(feature, cotangent, long_filter, taps, *tables(N))


def body(feature, cotangent, long_filter, short_filter, skip_gain):
    rep, grp, seq = lax.axis_index("rep"), lax.axis_index("grp"), lax.axis_index("seq")
    first = rep * 1024 + seq % Z * 128 + (grp * 4 + seq // Z) * 8
    taps = jnp.concatenate([short_filter, skip_gain[:, None]], 1)
    taps = lax.dynamic_slice_in_dim(taps, first, 8, 0)
    shape = (R, Z, V, 8, N)
    grad, filt, sums = run(
        feature.reshape(shape), cotangent.reshape(shape), long_filter.reshape(shape), taps
    )
    sums = sums[:, 0, :Z * 8].reshape(R, V, Z, 8).transpose(0, 2, 1, 3).reshape(-1)
    return grad.reshape(1, -1, N), filt.reshape(-1, N).astype(F32), sums


def solution(mesh):
    return jax.shard_map(
        body,
        mesh=mesh,
        in_specs=(
            P("rep", None, ("grp", "seq")),
            P("rep", None, ("grp", "seq")),
            P(None, ("grp", "seq")),
            P(),
            P(),
        ),
        out_specs=(P("rep", None, ("grp", "seq")), P("rep", ("grp", "seq")), P()),
        check_vma=False,
    )
```

time: 269 us -> 140 us (0.52)
  blocking collectives: 133 us -> 0 us
  Pallas kernels: 14.4 us -> 130 us
  waiting for transfers between devices: 60.6 us -> 0 us
  starting transfers between devices: 39.3 us -> 0 us
  local copies, waits for them, and re-layouts: 11.9 us -> 5.38 us
  other arithmetic: 6.7 us -> 2.97 us
    pallas_call x1, Pallas kernels: 14.4 us -> 130 us  [run(): pl.pallas_call(kernel, out_shape=(jax.ShapeDtypeStruct((R, Z, V, 8, N), B...]
    unnamed x1 -> x0, blocking collectives: 112 us -> none
    all_to_all x3 -> x0, waiting for transfers between devices: 60.6 us -> none  [the longest x1 51.2 us: body(): x = lax.all_to_all(both, ('grp', 'seq', 'rep'), 0, 0, tiled=True)]
    all_to_all x3 -> x0, starting transfers between devices: 39.3 us -> none  [the longest x1 18.6 us: body(): lax.all_to_all(filt, ('grp', 'seq'), 0, 0, tiled=True).reshape(64, 16, 128)]
    all_to_all x1 -> x0, blocking collectives: 20.9 us -> none  [body(): lax.all_to_all(fg.reshape(128, 8, 128), ('grp', 'seq'), 0, 0, tiled=True)]
    unnamed x22 -> x10, local copies, waits for them, and re-layouts: 8.08 us -> 4.28 us
  transfers between devices with their start and end apart: 3 -> 0, of which waited for: 2 -> 0; matrix products, arithmetic and copies ran while one was open for 4% -> 0% of each run, Pallas kernels for 0% -> 0%
where the time goes in v1:
time: 140 us; the launch traced here: 139 us
  Pallas kernels  130 us (93%)
  local copies, waits for them, and re-layouts  5.38 us (4%)
  other arithmetic  2.97 us (2%)
    pallas_call x1, Pallas kernels, run(): pl.pallas_call(kernel, out_shape=(jax.ShapeDtypeStruct((R, Z, V, 8, N), B...  130 us
    unnamed x10, local copies, waits for them, and re-layouts  4.28 us

profile of v1, /device:TPU:1, one launch (start us, length us, event | category | flops | bytes accessed | tf_op | source)
XLA Modules:
  0.0 138.9 jit_solution(232627503774242510)
XLA Ops:
  0.6 0.0 copy-start.3
  0.6 0.0 copy-start
  0.7 0.8 copy-done.3
  1.5 0.7 fusion.30
  2.2 0.1 copy.16.taps_ref
  2.3 0.3 fusion.27
  2.5 0.3 negate_convert_fusion
  2.9 0.8 fusion.28
  3.7 0.0 copy-done
  3.7 0.0 copy-start.1
  3.7 1.2 copy-done.1
  5.0 0.0 copy-start.2
  5.0 1.2 copy-done.2
  6.2 129.8 %shard_map.76 = (bf16[4,8,16,8,128]{4,3,2,1,0:T(8,128)(2,1)S(1)}, bf16[8,16,8,128]{3,2,1,0:T(8,128)(2,1)S(1)}, f32[64,1,128]{2,1,0:T(1,128)S(1)}) custom-call(bf16[4,8,16,8,128]{4,3,2,1,0:T(8,128)(2,1)S(1)} %bitcast.15, bf16[4,8,16,8,128]{4,3,2,1,0:T(8,128)(2,1)S(1)} %bitcast.16, bf16[4,8,16,8,128]{4,3,2,1,0:T(8,128)(2,1)S(1)} %bitcast.17, ...), custom_call_target="tpu_custom_call" | custom-call | tf_op jit(solution)/shard_map/pallas_call | solution.py:377
  136.0 0.1 copy.14
  136.1 0.1 reshape_squeeze.3
  136.2 0.1 copy.15
  136.4 0.8 reshape.33
  137.1 0.8 bitcast_convert_fusion
  138.0 1.0 copy.18
  (4 shorter events, 0.0 us)
Async XLA Ops:
  0.6 0.8 copy-start.3
  0.6 3.1 %copy-start = (bf16[1,4096,128]{2,1,0:T(8,128)(2,1)S(1)}, bf16[1,4096,128]{2,1,0:T(8,128)(2,1)}, u32[]{:S(2)}) copy-start(bf16[1,4096,128]{2,1,0:T(8,128)(2,1)} %param.5) | copy-start | bytes 3145732
  3.7 1.2 copy-start.1
  5.0 1.2 copy-start.2

commit v2 on v0

v2 whole, which is shorter than its diff:
```python
import math

import jax
import jax.numpy as jnp
import ml_dtypes
import numpy as np
from jax import lax
from jax.experimental import pallas as pl
from jax.experimental.pallas import tpu as pltpu
from jax.sharding import PartitionSpec as P

MESH = pl.DeviceIdType.MESH
rem, div = lax.rem, lax.div
Z, V, R = 8, 16, 4
W = R * V
N = 128
F32, BF = jnp.float32, jnp.bfloat16
ZORDER = (4, 3, 5, 2, 6, 1, 7)
MIX = 27
LIMIT = 60
H1, H2, C0, F0, G1, G2, O0, S1, S2, S3 = 0, 1, 2, 6, 10, 11, 12, 16, 17, 18


def tables(n):
    p = np.arange(n)

    def cis(num, den):
        angle = (num % den) * (2.0 * math.pi / den)
        return np.cos(angle), -np.sin(angle)

    quarter = 4 * p + 1
    o_re, o_im = cis(quarter[:, None] * p[None, :], 4 * n)
    t_re, t_im = cis(quarter[:, None] * p[None, :], 4 * n * n)
    i_re, i_im = cis(p[:, None] * p[None, :], n)
    fwd_outer = np.concatenate([o_re, o_im], 0)
    fwd_inner = np.block([[i_re, i_im], [-i_im, i_re]])
    inv_inner = np.block([[i_re, -i_im], [i_im, i_re]])
    inv_outer = np.concatenate([o_re.T, o_im.T], 1) / (n * n)
    half = ml_dtypes.bfloat16
    return (
        fwd_outer.astype(half), t_re.astype(np.float32), t_im.astype(np.float32),
        fwd_inner.astype(half), inv_inner.astype(half), inv_outer.astype(half),
    )


def place():
    g = lax.axis_index("grp")
    s = lax.axis_index("seq")
    r = lax.axis_index("rep")
    return g, div(r, 2) * 4 + div(s, Z), rem(s, Z), rem(r, 2)


def z_mate(k, me):
    to = rem(me[2] + k, Z)
    return to, {"seq": rem(me[1], 4) * Z + to}


def plane_device(x, y, core, me):
    return {"grp": x, "seq": rem(y, 4) * Z + me[2], "rep": div(y, 4) * 2 + core}


def core_mate(k, core, me):
    x = rem(me[0] + rem(k, 4), 4)
    y = rem(me[1] + div(k, 4), 8)
    return div(y, 4), x * 4 + rem(y, 4), plane_device(x, y, core, me)


def v_mate(k, me):
    x = rem(me[0] + rem(k, 4), 4)
    low = rem(rem(me[1], 4) + div(k, 4), 4)
    return x * 4 + low, {"grp": x, "seq": low * Z + me[2]}


def each(lo, hi, f):
    def step(k, carry):
        f(k)
        return carry

    lax.fori_loop(lo, hi, step, 0)


def y_device(k, me):
    y = rem(me[1] + k, 8)
    return {"seq": rem(y, 4) * Z + me[2], "rep": div(y, 4) * 2 + me[3]}


def xc_device(k, me):
    return {"grp": rem(me[0] + rem(k, 4), 4), "rep": div(me[1], 4) * 2 + rem(me[3] + div(k, 4), 2)}


def r_mate(k, me):
    r = rem(div(me[1], 4) * 2 + me[3] + k, R)
    return r, {"rep": r}


def signal(sem, device):
    pl.semaphore_signal(sem, inc=1, device_id=device, device_id_type=MESH)


def greet(me, gate):
    barrier = pltpu.get_barrier_semaphore()
    each(1, Z, lambda k: signal(barrier, z_mate(k, me)[1]))
    each(1, 8, lambda k: signal(barrier, xc_device(k, me)))
    each(1, 8, lambda k: signal(barrier, y_device(k, me)))
    pl.semaphore_wait(barrier, 21)
    each(1, 8, lambda k: signal(gate, xc_device(k, me)))


def done(ref, sem):
    pltpu.make_async_copy(ref, ref, sem).wait()


class Links:
    def __init__(self, me, send, recv, loc):
        self.me, self.send, self.recv, self.loc = me, send, recv, loc
        self.z, self.core = me[2], me[3]
        self.v = me[0] * 4 + rem(me[1], 4)
        self.high = div(me[1], 4)
        self.r = self.high * 2 + self.core

    def remote(self, src, dst, i, device):
        pltpu.make_async_remote_copy(
            src, dst, self.send.at[i], self.recv.at[i], device_id=device, device_id_type=MESH
        ).start()

    def local(self, src, dst, i):
        copy = pltpu.make_async_copy(src, dst, self.loc.at[i])
        copy.start()
        return copy


def shifted(values, m):
    lane = lax.broadcasted_iota(jnp.int32, (N, N), 1)
    row = lax.broadcasted_iota(jnp.int32, (N, N), 0)
    here = pltpu.roll(values, N - m, 1)
    below = jnp.where(row == N - 1, 0.0, pltpu.roll(here, N - 1, 0))
    return jnp.where(lane >= N - m, below, here)


class Exchange:
    def __init__(self, links, base, for_zero, for_one, ia, ib, dst, tally):
        self.ln, self.base = links, base
        self.for_zero, self.for_one = for_zero, for_one
        self.ia, self.ib, self.dst, self.tally = ia, ib, dst, tally

    def first_z(self):
        ln = self.ln
        for k in ZORDER:
            to, device = z_mate(k, ln.me)
            ln.remote(self.for_zero(to), self.ia.at[ln.z], self.base, device)

    def first_plane(self):
        ln = self.ln

        def one(k):
            high, v, device = core_mate(rem(k * MIX, W // 2), 1, ln.me)
            ln.remote(self.for_one(high, v), self.ib.at[ln.r, ln.v], self.base + 2, device)

        each(ln.core, W // 2, one)

    def own_first(self):
        ln = self.ln
        ln.local(self.for_zero(ln.z), self.ia.at[ln.z], 0).wait()

        @pl.when(ln.core == 1)
        def _():
            ln.local(self.for_one(ln.high, ln.v), self.ib.at[ln.r, ln.v], 1).wait()

    def second(self):
        ln = self.ln
        done(self.ia.at[pl.ds(0, Z - 1)], ln.recv.at[self.base])

        def one(k):
            high, v, device = core_mate(rem(k * MIX, W // 2), 0, ln.me)
            ln.remote(self.ia.at[:, high, v], self.dst.at[ln.r, :, ln.v], self.base + 1, device)

        each(1 - ln.core, W // 2, one)

        @pl.when(ln.core == 0)
        def _():
            ln.local(self.ia.at[:, ln.high, ln.v], self.dst.at[ln.r, :, ln.v], 0).wait()

        @pl.when(ln.core == 1)
        def _():
            done(self.tally.at[pl.ds(0, W - 1)], ln.recv.at[self.base + 2])
            for k in ZORDER:
                to, device = z_mate(k, ln.me)
                ln.remote(self.ib.at[:, :, to], self.dst.at[:, ln.z], self.base + 3, device)
            ln.local(self.ib.at[:, :, ln.z], self.dst.at[:, ln.z], 1).wait()

    def arrived(self):
        ln = self.ln

        @pl.when(ln.core == 0)
        def _():
            done(self.tally.at[pl.ds(0, W - 1)], ln.recv.at[self.base + 1])

        @pl.when(ln.core == 1)
        def _():
            done(self.tally.at[:, pl.ds(0, Z - 1)], ln.recv.at[self.base + 3])

    def sent(self):
        ln = self.ln
        done(self.ia.at[pl.ds(0, Z - 1)], ln.send.at[self.base])

        @pl.when(ln.core == 0)
        def _():
            done(self.tally.at[pl.ds(0, W // 2)], ln.send.at[self.base + 2])
            done(self.tally.at[pl.ds(0, W // 2 - 1)], ln.send.at[self.base + 1])

        @pl.when(ln.core == 1)
        def _():
            done(self.tally.at[pl.ds(0, W // 2 - 1)], ln.send.at[self.base + 2])
            done(self.tally.at[pl.ds(0, W // 2)], ln.send.at[self.base + 1])
            done(self.tally.at[:, pl.ds(0, Z - 1)], ln.send.at[self.base + 3])


class SmallExchange:
    def __init__(self, links, base, src, ih, dst):
        self.ln, self.base, self.src, self.ih, self.dst = links, base, src, ih, dst

    def first(self):
        ln = self.ln
        for k in ZORDER:
            to, device = z_mate(k, ln.me)
            ln.remote(self.src(to), self.ih.at[ln.z], self.base, device)

    def own_first(self):
        self.ln.local(self.src(self.ln.z), self.ih.at[self.ln.z], 2).wait()

    def second(self):
        ln = self.ln
        done(self.ih.at[pl.ds(0, Z - 1)], ln.recv.at[self.base])

        def one(k):
            to, device = v_mate(k, ln.me)
            ln.remote(self.ih.at[:, to], self.dst.at[:, ln.v], self.base + 1, device)

        each(1, V, one)
        ln.local(self.ih.at[:, ln.v], self.dst.at[:, ln.v], 2).wait()

    def arrived(self):
        done(self.dst.at[:, pl.ds(0, V - 1)], self.ln.recv.at[self.base + 1])

    def sent(self):
        done(self.ih.at[pl.ds(0, Z - 1)], self.ln.send.at[self.base])
        done(self.dst.at[:, pl.ds(0, V - 1)], self.ln.send.at[self.base + 1])


class Sums:
    def __init__(self, links, sk, sv, mid, si, dst):
        self.ln, self.sk, self.sv, self.mid, self.si, self.dst = links, sk, sv, mid, si, dst

    def first(self):
        ln = self.ln

        def one(k):
            ln.remote(self.sk, self.sv.at[ln.v], S1, v_mate(k, ln.me)[1])

        each(1, V, one)
        ln.local(self.sk, self.sv.at[ln.v], 0).wait()

    def second(self):
        ln = self.ln
        done(self.sv.at[pl.ds(0, V - 1)], ln.recv.at[S1])
        self.mid[...] = jnp.sum(self.sv[...], axis=0)
        for k in ZORDER:
            ln.remote(self.mid, self.si.at[ln.z], S2, z_mate(k, ln.me)[1])
        ln.local(self.mid, self.si.at[ln.z], 0).wait()

    def third(self):
        ln = self.ln
        done(self.si.at[pl.ds(0, Z - 1)], ln.recv.at[S2])
        for k in range(1, R):
            ln.remote(self.si, self.dst.at[ln.r], S3, r_mate(k, ln.me)[1])
        ln.local(self.si, self.dst.at[ln.r], 0).wait()

    def finish(self):
        ln = self.ln
        done(self.sv.at[pl.ds(0, V - 1)], ln.send.at[S1])
        done(self.si.at[pl.ds(0, Z - 1)], ln.send.at[S2])
        done(self.dst.at[pl.ds(0, R - 1)], ln.send.at[S3])
        done(self.dst.at[pl.ds(0, R - 1)], ln.recv.at[S3])


def spread(dst, src):
    def one(q):
        r, v = div(q, V), rem(q, V)
        for z in range(Z):
            at = pl.multiple_of(r * 8 * N + v * Z * 8 + z * 8, 8)
            dst[pl.ds(at, 8), :] = src[r, z, v].astype(F32)

    each(0, W, one)


def twisted(bs, first, tr, ti, count):
    for s in range(count):
        re, im = first[:N, s * N:(s + 1) * N], first[N:, s * N:(s + 1) * N]
        bs[s * N:(s + 1) * N, :N] = (re * tr - im * ti).astype(BF)
        bs[s * N:(s + 1) * N, N:] = (re * ti + im * tr).astype(BF)


def untwisted(zs, back, tr, ti, count):
    for s in range(count):
        re, im = back[s * N:(s + 1) * N, :N], back[s * N:(s + 1) * N, N:]
        zs[:N, s * N:(s + 1) * N] = (re * tr + im * ti).astype(BF)
        zs[N:, s * N:(s + 1) * N] = (im * tr - re * ti).astype(BF)


def input_part(cx, hx, taps_ref, tabs, oa, ob, spec_c, cs, hs, os, ds, bs, ys, zs):
    fo_ref, tr_ref, ti_ref, fi_ref, ii_ref, io_ref = tabs
    spread(cs, cx)

    def expand_h(v):
        for z in range(Z):
            hs[pl.ds(pl.multiple_of(v * Z * 8 + z * 8, 8), 8), :] = hx[z, v].astype(F32)

    each(0, V, expand_h)

    def channel(c):
        for b in range(R):
            ds[:, b * N:(b + 1) * N] = cs[pl.ds(b * 8 * N + c, N, stride=8), :].astype(BF)
        ds[:, R * N:] = hs[pl.ds(c, N, stride=8), :].astype(BF)
        tr, ti = tr_ref[...], ti_ref[...]
        first = jnp.dot(fo_ref[...], ds[...], preferred_element_type=F32)
        twisted(bs, first, tr, ti, R + 1)
        spec = jnp.dot(bs[...], fi_ref[...], preferred_element_type=F32)
        spec_c[c] = spec[:R * N]
        h_re, h_im = spec[R * N:, :N], spec[R * N:, N:]
        for b in range(R):
            c_re, c_im = spec[b * N:(b + 1) * N, :N], spec[b * N:(b + 1) * N, N:]
            ys[b * N:(b + 1) * N, :N] = (h_re * c_re + h_im * c_im).astype(BF)
            ys[b * N:(b + 1) * N, N:] = (h_re * c_im - h_im * c_re).astype(BF)
        back = jnp.dot(ys[...], ii_ref[...], preferred_element_type=F32)
        untwisted(zs, back, tr, ti, R)
        out = jnp.dot(io_ref[...], zs[...], preferred_element_type=F32)
        for b in range(R):
            cot = cs[pl.ds(b * 8 * N + c, N, stride=8), :]
            grad = out[:, b * N:(b + 1) * N] + taps_ref[c, 3] * cot
            res = (
                taps_ref[c, 0] * grad
                + taps_ref[c, 1] * shifted(grad, 1)
                + taps_ref[c, 2] * shifted(grad, 2)
            )
            os[pl.ds(b * 8 * N + c, N, stride=8), :] = res

    each(0, 8, channel)

    def pack(q):
        high, v = div(q, V), rem(q, V)
        base = high * 16 * N + v * Z * 8
        for z in range(Z):
            oa[z, high, v] = os[pl.ds(pl.multiple_of(base + z * 8, 8), 8), :].astype(BF)
        base = base + 8 * N
        ob[high, v] = os[pl.ds(pl.multiple_of(base, 64), 64), :].reshape(Z, 8, N).astype(BF)

    each(0, W // 2, pack)


def sums_part(links, fx, cs, fs, sk):
    def one(q, total):
        r, v = div(q, V), rem(q, V)
        for z in range(Z):
            at = pl.ds(pl.multiple_of(r * 8 * N + v * Z * 8 + z * 8, 8), 8)
            feat = fx[r, z, v].astype(F32)
            fs[at, :] = feat
            total = total + feat * cs[at, :]
        return total

    total = lax.fori_loop(0, W, one, jnp.zeros((8, N), F32))
    total = jnp.sum(total, axis=1, keepdims=True)
    lane = lax.broadcasted_iota(jnp.int32, (8, N), 1)
    spot = lax.broadcasted_iota(jnp.int32, (8, N), 0) + links.v * 8
    sk[...] = jnp.sum(jnp.where(lane == spot, total, 0.0), axis=0, keepdims=True)


def filter_part(tabs, go, spec_c, fs, gs, ds, bs, ys, zs):
    fo_ref, tr_ref, ti_ref, fi_ref, ii_ref, io_ref = tabs

    def channel(c):
        for b in range(R):
            ds[:, b * N:(b + 1) * N] = fs[pl.ds(b * 8 * N + c, N, stride=8), :].astype(BF)
        tr, ti = tr_ref[...], ti_ref[...]
        first = jnp.dot(fo_ref[...], ds[:, :R * N], preferred_element_type=F32)
        twisted(bs, first, tr, ti, R)
        spec = jnp.dot(bs[:R * N, :], fi_ref[...], preferred_element_type=F32)
        g_re = jnp.zeros((N, N), F32)
        g_im = jnp.zeros((N, N), F32)
        for b in range(R):
            f_re, f_im = spec[b * N:(b + 1) * N, :N], spec[b * N:(b + 1) * N, N:]
            c_re = spec_c[c, b * N:(b + 1) * N, :N]
            c_im = spec_c[c, b * N:(b + 1) * N, N:]
            g_re += f_re * c_re + f_im * c_im
            g_im += f_re * c_im - f_im * c_re
        ys[:N, :N] = g_re.astype(BF)
        ys[:N, N:] = g_im.astype(BF)
        back = jnp.dot(ys[:N, :], ii_ref[...], preferred_element_type=F32)
        untwisted(zs, back, tr, ti, 1)
        out = jnp.dot(io_ref[...], zs[:, :N], preferred_element_type=F32)
        gs[pl.ds(c, N, stride=8), :] = out

    each(0, 8, channel)

    def pack(v):
        for z in range(Z):
            go[z, v] = gs[pl.ds(pl.multiple_of(v * Z * 8 + z * 8, 8), 8), :].astype(BF)

    each(0, V, pack)


def kernel(
    f_ref, c_ref, h_ref, taps_ref, fo_ref, tr_ref, ti_ref, fi_ref, ii_ref, io_ref,
    out, out_g, out_s,
    ic, jc, if_, jf, io, jo, ih, ig, cx, fx, hx, oa, ob, go, tally,
    spec_c, cs, fs, hs, os, gs, ds, bs, ys, zs,
    sk, sv, mid, si, gate, send, recv, loc,
):
    me = place()
    tabs = (fo_ref, tr_ref, ti_ref, fi_ref, ii_ref, io_ref)
    ln = Links(me, send, recv, loc)
    filt = SmallExchange(ln, H1, lambda z: h_ref.at[ln.r, z], ih, hx)
    cot = Exchange(
        ln, C0, lambda z: c_ref.at[:, 0, z], lambda y, v: c_ref.at[y, 1, :, v], ic, jc, cx, tally
    )
    feat = Exchange(
        ln, F0, lambda z: f_ref.at[:, 0, z], lambda y, v: f_ref.at[y, 1, :, v], if_, jf, fx, tally
    )
    grad = Exchange(ln, O0, lambda z: oa.at[z], lambda y, v: ob.at[y, v], io, jo, out, tally)
    fgrad = SmallExchange(ln, G1, lambda z: go.at[z], ig, out_g)
    sums = Sums(ln, sk, sv, mid, si, out_s)

    greet(me, gate)
    filt.first()
    cot.first_z()
    pl.semaphore_wait(gate, 7)
    cot.first_plane()
    filt.own_first()
    cot.own_first()
    filt.second()
    cot.second()
    feat.first_z()
    feat.first_plane()
    feat.own_first()
    filt.arrived()
    cot.arrived()
    input_part(cx, hx, taps_ref, tabs, oa, ob, spec_c, cs, hs, os, ds, bs, ys, zs)
    feat.second()
    grad.first_z()
    grad.first_plane()
    grad.own_first()
    feat.arrived()
    sums_part(ln, fx, cs, fs, sk)
    sums.first()
    filter_part(tabs, go, spec_c, fs, gs, ds, bs, ys, zs)
    fgrad.first()
    fgrad.own_first()
    sums.second()
    grad.second()
    fgrad.second()
    sums.third()
    for each_one in (filt, cot, feat, grad, fgrad):
        each_one.sent()
    grad.arrived()
    fgrad.arrived()
    sums.finish()


def run(feature, cotangent, long_filter, taps):
    def bf(*shape):
        return pltpu.VMEM(shape + (8, N), BF)

    def f32(*shape):
        return pltpu.VMEM(shape, F32)

    vm = pl.BlockSpec(memory_space=pltpu.VMEM)
    whole = pl.BlockSpec(memory_space=pl.ANY)
    return pl.pallas_call(
        kernel,
        out_shape=(
            jax.ShapeDtypeStruct((R, Z, V, 8, N), BF),
            jax.ShapeDtypeStruct((Z, V, 8, N), BF),
            jax.ShapeDtypeStruct((R, Z, 1, N), F32),
        ),
        in_specs=[whole] * 3 + [pl.BlockSpec(memory_space=pltpu.SMEM)] + [vm] * 6,
        out_specs=(vm, vm, vm),
        scratch_shapes=[
            bf(Z, 2, V), bf(R, V, Z), bf(Z, 2, V), bf(R, V, Z), bf(Z, 2, V), bf(R, V, Z),
            bf(Z, V), bf(Z, V), bf(R, Z, V), bf(R, Z, V), bf(Z, V),
            bf(Z, 2, V), bf(2, V, Z), bf(Z, V), bf(W, Z),
            f32(8, R * N, 2 * N), f32(W * Z * 8, N), f32(W * Z * 8, N), f32(V * Z * 8, N),
            f32(W * Z * 8, N), f32(V * Z * 8, N),
            pltpu.VMEM((N, 5 * N), BF), pltpu.VMEM((5 * N, 2 * N), BF),
            pltpu.VMEM((4 * N, 2 * N), BF), pltpu.VMEM((2 * N, 4 * N), BF),
            f32(1, N), f32(V, 1, N), f32(1, N), f32(Z, 1, N),
            pltpu.SemaphoreType.REGULAR,
            pltpu.SemaphoreType.DMA((19,)), pltpu.SemaphoreType.DMA((19,)), pltpu.SemaphoreType.DMA((3,)),
        ],
        compiler_params=pltpu.CompilerParams(
            collective_id=0, has_side_effects=True, vmem_limit_bytes=LIMIT << 20
        ),
    )(feature, cotangent, long_filter, taps, *tables(N))


def body(feature, cotangent, long_filter, short_filter, skip_gain):
    rep, grp, seq = lax.axis_index("rep"), lax.axis_index("grp"), lax.axis_index("seq")
    first = rep * 1024 + seq % Z * 128 + (grp * 4 + seq // Z) * 8
    taps = jnp.concatenate([short_filter, skip_gain[:, None]], 1)
    taps = lax.dynamic_slice_in_dim(taps, first, 8, 0)
    pairs = (2, 2, Z, V, 8, N)
    grad, filt, sums = run(
        feature.reshape(pairs), cotangent.reshape(pairs), long_filter.reshape(R, Z, V, 8, N), taps
    )
    return grad.reshape(1, -1, N), filt.reshape(-1, N).astype(F32), sums.reshape(-1)


def solution(mesh):
    return jax.shard_map(
        body,
        mesh=mesh,
        in_specs=(
            P("rep", None, ("grp", "seq")),
            P("rep", None, ("grp", "seq")),
            P(None, ("grp", "seq")),
            P(),
            P(),
        ),
        out_specs=(P("rep", None, ("grp", "seq")), P("rep", ("grp", "seq")), P()),
        check_vma=False,
    )
```

time: 269 us -> 117 us (0.43)
  blocking collectives: 133 us -> 0 us
  Pallas kernels: 14.4 us -> 109 us
  waiting for transfers between devices: 60.6 us -> 0 us
  starting transfers between devices: 39.3 us -> 0 us
  local copies, waits for them, and re-layouts: 11.9 us -> 4.36 us
  other arithmetic: 6.7 us -> 1.85 us
    unnamed x1 -> x0, blocking collectives: 112 us -> none
    pallas_call x1, Pallas kernels: 14.4 us -> 109 us  [run(): pl.pallas_call(kernel, out_shape=(jax.ShapeDtypeStruct((R, Z, V, 8, N), B...]
    all_to_all x3 -> x0, waiting for transfers between devices: 60.6 us -> none  [the longest x1 51.2 us: body(): x = lax.all_to_all(both, ('grp', 'seq', 'rep'), 0, 0, tiled=True)]
    all_to_all x3 -> x0, starting transfers between devices: 39.3 us -> none  [the longest x1 18.6 us: body(): lax.all_to_all(filt, ('grp', 'seq'), 0, 0, tiled=True).reshape(64, 16, 128)]
    all_to_all x1 -> x0, blocking collectives: 20.9 us -> none  [body(): lax.all_to_all(fg.reshape(128, 8, 128), ('grp', 'seq'), 0, 0, tiled=True)]
    unnamed x22 -> x9, local copies, waits for them, and re-layouts: 8.08 us -> 4.36 us
  transfers between devices with their start and end apart: 3 -> 0, of which waited for: 2 -> 0; matrix products, arithmetic and copies ran while one was open for 4% -> 0% of each run, Pallas kernels for 0% -> 0%
where the time goes in v2:
time: 117 us; the launch traced here: 116 us
  Pallas kernels  109 us (93%)
  local copies, waits for them, and re-layouts  4.36 us (4%)
  other arithmetic  1.85 us (2%)
    pallas_call x1, Pallas kernels, run(): pl.pallas_call(kernel, out_shape=(jax.ShapeDtypeStruct((R, Z, V, 8, N), B...  109 us
    unnamed x9, local copies, waits for them, and re-layouts  4.36 us

profile of v2, /device:TPU:1, one launch (start us, length us, event | category | flops | bytes accessed | tf_op | source)
XLA Modules:
  0.0 116.4 jit_solution(1607435368533040773)
XLA Ops:
  0.6 0.0 copy-start
  0.7 0.0 copy-start.2
  0.7 0.8 copy-done
  1.5 0.0 copy-done.2
  1.5 0.1 fusion
  1.5 0.7 copy.18.taps_ref
  2.2 109.5 %shard_map.130 = (bf16[4,8,16,8,128]{4,3,2,1,0:T(8,128)(2,1)}, bf16[8,16,8,128]{3,2,1,0:T(8,128)(2,1)}, f32[4,8,1,128]{3,2,1,0:T(1,128)}) custom-call(bf16[2,2,8,16,8,128]{5,4,3,2,1,0:T(8,128)(2,1)} %bitcast.10, bf16[2,2,8,16,8,128]{5,4,3,2,1,0:T(8,128)(2,1)} %bitcast.11, bf16[4,8,16,8,128]{4,3,2,1,0:T(8,128)(2,1)} %bitcast.12, f32[8,4]{1,0:T(8,128)} %copy.18.taps_ref, ...), custom_call_target="tpu_custom_call" | custom-call | tf_op jit(solution)/shard_map/pallas_call | solution.py:477
  111.7 1.8 %bitcast_convert_fusion = f32[1024,128]{1,0:T(8,128)} fusion(bf16[8,16,8,128]{3,2,1,0:T(8,128)(2,1)} %get-tuple-element.7), kind=kLoop, calls=%fused_computation | loop fusion | flops 131072 | bytes 786432 | tf_op jit(solution)/shard_map/convert_element_type | solution.py:513
  113.5 0.0 copy-start.1
  113.5 2.3 %copy.21 = bf16[1,4096,128]{2,1,0:T(8,128)(2,1)} copy(bf16[1,4096,128]{2,1,0:T(8,128)(2,1)} %bitcast.9) | data formatting | bytes 2097152
  115.8 0.0 copy-done.1
  115.8 0.6 copy.22
Async XLA Ops:
  0.6 0.8 copy-start
  0.7 0.8 copy-start.2
  113.5 2.3 %copy-start.1 = (f32[4,8,1,128]{3,2,1,0:T(1,128)S(1)}, f32[4,8,1,128]{3,2,1,0:T(1,128)}, u32[]{:S(2)}) copy-start(f32[4,8,1,128]{3,2,1,0:T(1,128)} %get-tuple-element.8) | copy-start | bytes 49156
